TPU v7x, 256 devices: a whole 4x4x8 slice. The times are simulated.
256 devices in a mesh: group: 8 (over y, core), dom: 32 (over z, x).
Axes of the slice: x: 4, y: 4, z: 8, core: 2. Of those that a mesh axis runs over, the one named last changes fastest.
Arguments:
- features: bfloat16 [131072, 256], P(('group', 'dom')), may hold values from -6 to 6
- preact: bfloat16 [131072, 256], P(('group', 'dom')), may hold values from -6 to 6
- agg_first: bfloat16 [131072, 256], P(('group', 'dom')), may hold values from -6 to 6
- agg_second: bfloat16 [131072, 256], P(('group', 'dom')), may hold values from -6 to 6
- grad_out: bfloat16 [131072, 256], P(('group', 'dom')), may hold values from -6 to 6
- self_first: bfloat16 [256, 256], replicated, may hold values from -0.375 to 0.375
- neigh_first: bfloat16 [256, 256], replicated, may hold values from -0.375 to 0.375
- self_second: bfloat16 [256, 256], replicated, may hold values from -0.375 to 0.375
- neigh_second: bfloat16 [256, 256], replicated, may hold values from -0.375 to 0.375
- tile_vals: bfloat16 [98304, 128, 128], P(('group', 'dom')), may hold values from -0.109375 to 0.109375
- tile_rows: int32 [256, 384], P(('group', 'dom')), may hold values from 0 to 15
- tile_cols: int32 [256, 384], P(('group', 'dom')), may hold values from 0 to 15
- tile_count: int32 [256], P(('group', 'dom')), may hold values from 96 to 384, as said below
- send_count: int32 [256, 32], P(('group', 'dom')), may hold values from 0 to 192, as said below
- mirror_slot: int32 [256, 32, 192], P(('group', 'dom')), may hold values from 0 to 2047, as said below
- master_row: int32 [256, 32, 192], P(('group', 'dom')), may hold values from 0 to 511
Outputs:
- input_grad: bfloat16 [131072, 256], P(('group', 'dom'))
- weight_grads: float32 [4, 256, 256], replicated
Inputs may be any that keep to these rules, and one draw needn't show every extreme that they name: `send_count`: the counts of each partition sum to 2048. In every group one partition, drawn per group, has exactly 192 rows from every partition of the group, its own included. `mirror_slot`: for each partition the entries c < send_count of its 32 lists together name each of its 2048 slots exactly once; the later entries are arbitrary slots. `master_row`: entries past the sender's count are arbitrary rows. `tile_count`: tiles at or past the count are padding with arbitrary contents. Some partition uses all 384 tiles, another only 96.
All inputs are finite; a program needn't handle non-finite values.
Results may differ from a plain program's by a relative error of at most 0.0095.
Values may be sent and summed in bfloat16 or wider, within the bound.
No kernel may reach another device: no remote copies, remote signals or barrier semaphores. Data moves between devices by JAX's collectives and lax.ppermute only.
A program may use at most 128 MiB of HBM per device.

v0:
```python
import math

import jax
import jax.numpy as jnp
from jax import lax
from jax.sharding import PartitionSpec as P

SLOTS = 2048


def spread_back(tile_vals, row_list, col_list, tile_total, mirrored):
    tiles_n = tile_vals.shape[0]
    tile_edge = tile_vals.shape[1]
    feat_width = mirrored.shape[1]
    blocks_n = mirrored.shape[0] // tile_edge
    blocks = mirrored.reshape(blocks_n, tile_edge, feat_width)
    step_tiles = math.gcd(32, tiles_n)
    turn_count = (tile_total + step_tiles - 1) // step_tiles

    def visit(turn_index, running):
        first = turn_index * step_tiles
        tile_block = lax.dynamic_slice_in_dim(tile_vals, first, step_tiles, 0)
        row_block = lax.dynamic_slice_in_dim(row_list, first, step_tiles, 0)
        col_block = lax.dynamic_slice_in_dim(col_list, first, step_tiles, 0)
        picked = blocks[row_block]
        product = jnp.einsum("tij,tif->tjf", tile_block, picked, preferred_element_type=jnp.float32)
        live_tiles = first + jnp.arange(step_tiles) < tile_total
        targets = jnp.where(live_tiles, col_block, blocks_n)
        return running.at[targets].add(product, mode="drop")

    running = lax.fori_loop(
        0, turn_count, visit, jnp.zeros((blocks_n, tile_edge, feat_width), jnp.float32)
    )
    return running.reshape(-1, feat_width)


def on_device(
    features,
    preact,
    agg_first,
    agg_second,
    grad_out,
    self_first,
    neigh_first,
    self_second,
    neigh_second,
    tile_vals,
    tile_rows,
    tile_cols,
    tile_count,
    send_count,
    mirror_slot,
    master_row,
):
    domains = lax.axis_size("dom")
    masters = features.shape[0]
    feat_width = features.shape[1]
    factor = (masters * domains * lax.axis_size("group")) ** (-0.5)
    slot_list = mirror_slot[0]
    row_list = master_row[0]
    counts = send_count[0]
    capacity = slot_list.shape[1]
    live_slots = jnp.arange(capacity)[None, :] < counts[:, None]
    slot_index = jnp.where(live_slots, slot_list, SLOTS)

    def mirror_round(pushed):
        outgoing = pushed[row_list]
        arrived = lax.all_to_all(outgoing, "dom", split_axis=0, concat_axis=0, tiled=True)
        mirrored = (
            jnp.zeros((SLOTS, feat_width), jnp.bfloat16)
            .at[slot_index.reshape(-1)]
            .set(arrived.reshape(-1, feat_width), mode="drop")
        )
        spread = spread_back(tile_vals, tile_rows[0], tile_cols[0], tile_count[0], mirrored).astype(
            jnp.bfloat16
        )
        leaving = jnp.where(live_slots[:, :, None], spread[slot_list], jnp.zeros((), jnp.bfloat16))
        landed = lax.all_to_all(leaving, "dom", split_axis=0, concat_axis=0, tiled=True)
        return (
            jnp.zeros((masters, feat_width), jnp.float32)
            .at[row_list.reshape(-1)]
            .add(landed.reshape(-1, feat_width).astype(jnp.float32))
        )

    def layer_back(inputs, stored, upstream, w_self, w_neigh):
        grad_self = jnp.einsum("nf,ng->fg", inputs, upstream, preferred_element_type=jnp.float32)
        grad_neigh = jnp.einsum("nf,ng->fg", stored, upstream, preferred_element_type=jnp.float32)
        pushed = jnp.einsum(
            "nf,gf->ng", upstream, w_neigh, preferred_element_type=jnp.float32
        ).astype(jnp.bfloat16)
        returned = mirror_round(pushed)
        layer_grad = (
            jnp.einsum("nf,gf->ng", upstream, w_self, preferred_element_type=jnp.float32) + returned
        )
        grad_self, grad_neigh = lax.psum((grad_self, grad_neigh), ("group", "dom"))
        return (layer_grad, grad_self, grad_neigh)

    activated = jnp.maximum(preact, 0.0)
    second_grad, self_two, neigh_two = layer_back(
        activated, agg_second, grad_out, self_second, neigh_second
    )
    first_upstream = jnp.where(preact > 0, second_grad, 0.0).astype(jnp.bfloat16)
    first_grad, self_one, neigh_one = layer_back(
        features, agg_first, first_upstream, self_first, neigh_first
    )
    weight_grads = jnp.stack([self_one, neigh_one, self_two, neigh_two]) * factor
    return (first_grad.astype(jnp.bfloat16), weight_grads)


def solution(mesh):
    in_specs = (
        P(("group", "dom"), None),
        P(("group", "dom"), None),
        P(("group", "dom"), None),
        P(("group", "dom"), None),
        P(("group", "dom"), None),
        P(),
        P(),
        P(),
        P(),
        P(("group", "dom"), None, None),
        P(("group", "dom"), None),
        P(("group", "dom"), None),
        P(("group", "dom")),
        P(("group", "dom"), None),
        P(("group", "dom"), None, None),
        P(("group", "dom"), None, None),
    )
    out_specs = (P(("group", "dom"), None), P())
    return jax.shard_map(
        on_device, mesh=mesh, in_specs=in_specs, out_specs=out_specs, check_vma=False
    )
```

profile of v0, /device:TPU:8, one launch (start us, length us, event | category | flops | bytes accessed | tf_op | source)
XLA Modules:
  0.0 1133.7 jit_solution(7949309984261849835)
XLA Ops:
  9.3 25.1 %gather_fusion.2 = bf16[6144,256]{1,0:T(8,128)(2,1)} fusion(bf16[512,256]{1,0:T(8,128)(2,1)S(1)} %convolution_convert_fusion.1, s32[6144]{0:T(1024)S(1)} %broadcast_clamp_fusion.1), kind=kCustom, calls=%fused_computation.2 | custom fusion | bytes 6316032 | tf_op jit(solution)/shard_map/gather | solution.py:67
  34.4 11.4 %all-to-all-start = ((bf16[32,192,256]{2,1,0:T(8,128)(2,1)}), bf16[32,192,256]{2,1,0:T(8,128)(2,1)S(1)}, u32[]{:S(2)}, u32[]{:S(2)}) async-start(bf16[32,192,256]{2,1,0:T(8,128)(2,1)} %bitcast.66), calls=%async_computation | async-start | bytes 6291456 | tf_op jit(solution)/shard_map/all_to_all | solution.py:68
  47.1 16.6 %copy.18 = bf16[384,128,128]{1,2,0:T(8,128)(2,1)} copy(bf16[384,128,128]{2,1,0:T(8,128)(2,1)} %param.29) | data formatting | bytes 25165824 | tf_op jit(solution)/shard_map/while | solution.py:31
  66.2 52.0 %all-to-all-done = bf16[32,192,256]{2,1,0:T(8,128)(2,1)S(1)} async-done(((bf16[32,192,256]{2,1,0:T(8,128)(2,1)}), bf16[32,192,256]{2,1,0:T(8,128)(2,1)S(1)}, u32[]{:S(2)}, u32[]{:S(2)}) %all-to-all-start) | async-done | bytes 3145760 | tf_op jit(solution)/shard_map/all_to_all | solution.py:68
  119.8 27.0 %scatter_custom_fusion.2 = bf16[2048,256]{1,0:T(8,128)(2,1)S(1)} fusion(s32[6144]{0:T(1024)S(1)} %bitcast.74, bf16[6144,256]{1,0:T(8,128)(2,1)} %bitcast.70, bf16[]{:T(256)} %constant.13.clone.1), kind=kCustom, calls=%fused_computation.42 | custom fusion | bytes 1049088 | tf_op jit(solution)/shard_map/scatter | solution.py:72
  146.9 145.1 %while.20 = (s32[]{:T(128)}, f32[16,128,256]{2,1,0:T(8,128)S(1)}, s32[]{:T(128)}, s32[]{:T(128)}, s32[384]{0:T(512)}, /*index=5*/bf16[384,128,128]{1,2,0:T(8,128...) while((s32[]{:T(128)}, f32[16,128,256]{2,1,0:T(8,128)S(1)}, ...), condition=%wide.region_3.4_spmd, body=%wide.region_1.3_spmd.sunk | while | flops 269485344 | bytes 24122428 | solution.py:31
  213.0 6.5 scatter_fusion
  256.5 6.5 scatter_fusion
  271.0 6.5 scatter_fusion
  292.1 25.1 %gather_fusion.3 = bf16[6144,256]{1,0:T(8,128)(2,1)} fusion(bf16[2048,256]{1,0:T(8,128)(2,1)S(1)} %bitcast.61, s32[6144]{0:T(1024)S(1)} %broadcast_clamp_fusion), kind=kCustom, calls=%fused_computation.3 | custom fusion | bytes 6316032 | tf_op jit(solution)/shard_map/gather | solution.py:77
  322.2 32.7 %all-to-all-start.1 = ((bf16[32,192,256]{2,1,0:T(8,128)(2,1)}), bf16[32,192,256]{2,1,0:T(8,128)(2,1)S(1)}, u32[]{:S(2)}, u32[]{:S(2)}) async-start(bf16[32,192,256]{2,1,0:T(8,128)(2,1)} %broadcast_select_fusion.1), calls=%async_computation.1 | async-start | bytes 6291456 | tf_op jit(solution)/shard_map/all_to_all | solution.py:78
  356.9 69.4 %all-to-all-done.1 = bf16[32,192,256]{2,1,0:T(8,128)(2,1)S(1)} async-done(((bf16[32,192,256]{2,1,0:T(8,128)(2,1)}), bf16[32,192,256]{2,1,0:T(8,128)(2,1)S(1)}, u32[]{:S(2)}, u32[]{:S(2)}) %all-to-all-start.1) | async-done | bytes 3145760 | tf_op jit(solution)/shard_map/all_to_all | solution.py:78
  426.3 35.4 %scatter_custom_fusion.3 = f32[512,256]{1,0:T(8,128)} fusion(f32[512,256]{1,0:T(8,128)} %fusion.17, s32[6144]{0:T(1024)S(1)} %bitcast.72, bf16[6144,256]{1,0:T(8,128)(2,1)S(1)} %bitcast.65), kind=kCustom, calls=%fused_computation.28 | custom fusion | flops 3145728 | bytes 3670016 | tf_op jit(solution)/shard_map/scatter-add | solution.py:82
  464.8 25.1 %gather_fusion.4 = bf16[6144,256]{1,0:T(8,128)(2,1)} fusion(bf16[512,256]{1,0:T(8,128)(2,1)S(1)} %convolution_convert_fusion, s32[6144]{0:T(1024)S(1)} %broadcast_clamp_fusion.1), kind=kCustom, calls=%fused_computation.4 | custom fusion | bytes 6316032 | tf_op jit(solution)/shard_map/gather | solution.py:67
  496.4 71.5 %all-to-all-done.2 = bf16[32,192,256]{2,1,0:T(8,128)(2,1)S(1)} async-done(((bf16[32,192,256]{2,1,0:T(8,128)(2,1)}), bf16[32,192,256]{2,1,0:T(8,128)(2,1)S(1)}, u32[]{:S(2)}, u32[]{:S(2)}) %all-to-all-start.2) | async-done | bytes 3145760 | tf_op jit(solution)/shard_map/all_to_all | solution.py:68
  569.6 26.9 %scatter_custom_fusion.4 = bf16[2048,256]{1,0:T(8,128)(2,1)S(1)} fusion(s32[6144]{0:T(1024)} %bitcast.75, bf16[6144,256]{1,0:T(8,128)(2,1)} %bitcast.71, bf16[]{:T(256)} %constant.13.clone.1), kind=kCustom, calls=%fused_computation.40 | custom fusion | bytes 1049088 | tf_op jit(solution)/shard_map/scatter | solution.py:72
  596.7 145.0 %while.21 = (s32[]{:T(128)}, f32[16,128,256]{2,1,0:T(8,128)S(1)}, s32[]{:T(128)}, s32[]{:T(128)}, s32[384]{0:T(512)}, /*index=5*/bf16[384,128,128]{1,2,0:T(8,128...) while((s32[]{:T(128)}, f32[16,128,256]{2,1,0:T(8,128)S(1)}, ...), condition=%wide.region_8.9_spmd, body=%wide.region_6.8_spmd.sunk | while | flops 269485344 | bytes 24122428 | solution.py:31
  662.7 6.5 scatter_fusion.1
  706.2 6.5 scatter_fusion.1
  720.8 6.5 scatter_fusion.1
  741.9 25.1 %gather_fusion.5 = bf16[6144,256]{1,0:T(8,128)(2,1)} fusion(bf16[2048,256]{1,0:T(8,128)(2,1)S(1)} %bitcast.60, s32[6144]{0:T(1024)S(1)} %broadcast_clamp_fusion), kind=kCustom, calls=%fused_computation.5 | custom fusion | bytes 6316032 | tf_op jit(solution)/shard_map/gather | solution.py:77
  771.9 32.1 %all-to-all-start.3 = ((bf16[32,192,256]{2,1,0:T(8,128)(2,1)}), bf16[32,192,256]{2,1,0:T(8,128)(2,1)S(1)}, u32[]{:S(2)}, u32[]{:S(2)}) async-start(bf16[32,192,256]{2,1,0:T(8,128)(2,1)} %broadcast_select_fusion), calls=%async_computation.3 | async-start | bytes 6291456 | tf_op jit(solution)/shard_map/all_to_all | solution.py:78
  814.0 270.6 %all-reduce.3.cloned.1.call-done = (f32[1,256,256]{1,2,0:T(8,128)}, f32[1,256,256]{1,2,0:T(8,128)}, f32[1,256,256]{1,2,0:T(8,128)}, f32[1,256,256]{1,2,0:T(8,128)}) async-done(((f32[1,256,256]{1,2,0:T(8,128)}, f32[1,256,256]{1,2,0:T(8,128)}, f32[1,256,256]{1,2,0:T(8,128)}, f32[1,256,256]{1,2,0:T(8,128)}), (f32[1,256,256]{1,2,0:T(8,128)}, f32[1,256,256]{1,2,0:T(8,128)}, f32[1,256,256]{1,2,0:T(8,128)}, ...) | async-done | bytes 1048592 | tf_op jit(solution)/shard_map/psum | solution.py:95
  1089.5 35.6 %scatter_custom_fusion.5 = f32[512,256]{1,0:T(8,128)} fusion(f32[512,256]{1,0:T(8,128)} %fusion.18, s32[6144]{0:T(1024)} %bitcast.73, bf16[6144,256]{1,0:T(8,128)(2,1)S(1)} %bitcast.64), kind=kCustom, calls=%fused_computation.26 | custom fusion | flops 3145728 | bytes 3670016 | tf_op jit(solution)/shard_map/scatter-add | solution.py:82
  (154 shorter events, 297.6 us)
Async XLA Ops:
  7.2 1.0 copy-start
  34.4 12.1 %copy-start.9 = (s32[1,384]{1,0:T(1,128)S(1)}, s32[1,384]{1,0:T(1,128)}, u32[]{:S(2)}) copy-start(s32[1,384]{1,0:T(1,128)} %param.31) | copy-start | bytes 4612
  34.4 83.7 %all-to-all-start = ((bf16[32,192,256]{2,1,0:T(8,128)(2,1)}), bf16[32,192,256]{2,1,0:T(8,128)(2,1)S(1)}, u32[]{:S(2)}, u32[]{:S(2)}) async-start(bf16[32,192,256]{2,1,0:T(8,128)(2,1)} %bitcast.66), calls=%async_computation | async-start | bytes 6291456 | tf_op jit(solution)/shard_map/all_to_all | solution.py:68
  47.1 16.7 %copy-start.10 = (s32[1,384]{1,0:T(1,128)S(1)}, s32[1,384]{1,0:T(1,128)}, u32[]{:S(2)}) copy-start(s32[1,384]{1,0:T(1,128)} %param.30) | copy-start | bytes 4612
  47.1 17.3 %copy-start.11 = (s32[1,32]{1,0:T(1,128)S(1)}, s32[1,32]{1,0:T(1,128)}, u32[]{:S(2)}) copy-start(s32[1,32]{1,0:T(1,128)} %param.33) | copy-start | bytes 388
  47.1 18.1 %copy-start.5 = (s32[1,32,192]{2,1,0:T(8,128)S(1)}, s32[1,32,192]{2,1,0:T(8,128)}, u32[]{:S(2)}) copy-start(s32[1,32,192]{2,1,0:T(8,128)} %param.34) | copy-start | bytes 73732
  66.2 80.8 %copy-start.8 = (s32[6144,1]{0,1:T(1,128)}, s32[6144,1]{0,1:T(1,128)S(1)}, u32[]{:S(2)}) copy-start(s32[6144,1]{0,1:T(1,128)S(1)} %compare_select_fusion.6) | copy-start | bytes 73732
  118.1 1.6 copy-start.2
  322.2 32.7 %copy-start.6 = (s32[1,32,192]{2,1,0:T(8,128)S(1)}, s32[1,32,192]{2,1,0:T(8,128)}, u32[]{:S(2)}) copy-start(s32[1,32,192]{2,1,0:T(8,128)} %param.35) | copy-start | bytes 73732
  322.2 104.2 %all-to-all-start.1 = ((bf16[32,192,256]{2,1,0:T(8,128)(2,1)}), bf16[32,192,256]{2,1,0:T(8,128)(2,1)S(1)}, u32[]{:S(2)}, u32[]{:S(2)}) async-start(bf16[32,192,256]{2,1,0:T(8,128)(2,1)} %broadcast_select_fusion.1), calls=%async_computation.1 | async-start | bytes 6291456 | tf_op jit(solution)/shard_map/all_to_all | solution.py:78
  356.9 133.0 %copy-start.7 = (s32[6144,1]{0,1:T(1,128)}, s32[6144,1]{0,1:T(1,128)S(1)}, u32[]{:S(2)}) copy-start(s32[6144,1]{0,1:T(1,128)S(1)} %compare_select_fusion.7) | copy-start | bytes 73732
  462.9 0.7 copy-start.1
  489.9 78.0 %all-to-all-start.2 = ((bf16[32,192,256]{2,1,0:T(8,128)(2,1)}), bf16[32,192,256]{2,1,0:T(8,128)(2,1)S(1)}, u32[]{:S(2)}, u32[]{:S(2)}) async-start(bf16[32,192,256]{2,1,0:T(8,128)(2,1)} %bitcast.67), calls=%async_computation.2 | async-start | bytes 6291456 | tf_op jit(solution)/shard_map/all_to_all | solution.py:68
  567.9 1.6 copy-start.3
  771.9 317.6 %all-to-all-start.3 = ((bf16[32,192,256]{2,1,0:T(8,128)(2,1)}), bf16[32,192,256]{2,1,0:T(8,128)(2,1)S(1)}, u32[]{:S(2)}, u32[]{:S(2)}) async-start(bf16[32,192,256]{2,1,0:T(8,128)(2,1)} %broadcast_select_fusion), calls=%async_computation.3 | async-start | bytes 6291456 | tf_op jit(solution)/shard_map/all_to_all | solution.py:78
  804.0 8.0 copy-start.4
  804.0 280.6 %all-reduce.3.cloned.1.call-start = ((), (), s32[]{:S(2)}) async-start(), calls=%async_computation.4 | async-start | bytes 2097152 | tf_op jit(solution)/shard_map/psum | solution.py:95
Sparse Core Ops, SparseCore 0:
  812.1 272.4 all-reduce.2
where the time goes:
time: 1140 us; the launch traced here: 1130 us
  waiting for transfers between devices  463 us (41%)
  other arithmetic  248 us (22%)
  local copies, waits for them, and re-layouts  219 us (19%)
  matrix products  105 us (9%)
  starting transfers between devices  82.7 us (7%)
  between operations  14.9 us (1%)
    psum x1, waiting for transfers between devices, layer_back(): grad_self, grad_neigh = lax.psum((grad_self, grad_neigh), ('group', 'dom'))  271 us
    scatter-add x20, other arithmetic, visit(): return running.at[targets].add(product, mode='drop')  130 us
    all_to_all x2, waiting for transfers between devices, mirror_round(): lax.all_to_all(outgoing, 'dom', split_axis=0, concat_axis=0, tiled=True)  123 us
    dot_general x20, matrix products, visit(): jnp.einsum('tij,tif->tjf', tile_block, picked, preferred_element_type=jnp...  91 us
    scatter-add x2, other arithmetic, mirror_round(): return jnp.zeros((masters, feat_width), jnp.float32).at[row_list.reshape(...  71 us
    all_to_all x2, waiting for transfers between devices, mirror_round(): lax.all_to_all(leaving, 'dom', split_axis=0, concat_axis=0, tiled=True)  69.4 us
    all_to_all x2, starting transfers between devices, mirror_round(): lax.all_to_all(leaving, 'dom', split_axis=0, concat_axis=0, tiled=True)  64.8 us
    scatter x2, local copies, waits for them, and re-layouts, mirror_round(): mirrored = jnp.zeros((SLOTS, feat_width), jnp.bfloat16).at[slot_index.res...  53.9 us
  transfers between devices with their start and end apart: 5, of which 4 were waited for; matrix products, arithmetic and copies ran while one was open for 3% of the time, Pallas kernels for 0%

commit v1 on v0

v1 whole, which is shorter than its diff:
```python
import functools

import jax
import jax.numpy as jnp
from jax import lax
from jax.experimental import pallas as pl
from jax.experimental.pallas import tpu as pltpu
from jax.sharding import PartitionSpec as P

SLOTS = 2048
EDGE = 128
KSTEP = 512
BF = jnp.bfloat16
F32 = jnp.float32
BIG = 56 * 1024 * 1024


def params():
    return pltpu.CompilerParams(vmem_limit_bytes=BIG)


def dot_nt(a, b):
    return lax.dot_general(a, b, (((1,), (1,)), ((), ())), preferred_element_type=F32)


def dot_nn(a, b):
    return lax.dot_general(a, b, (((1,), (0,)), ((), ())), preferred_element_type=F32)


def wide_onehot(index_row, height):
    iota = lax.broadcasted_iota(jnp.int32, (height, index_row.shape[1]), 0).astype(F32)
    return jnp.where(iota == index_row, 1.0, 0.0).astype(BF)


def tall_onehot(index_row, width):
    column = jnp.transpose(jnp.broadcast_to(index_row, (EDGE, EDGE)))
    parts = []
    for b in range(width // EDGE):
        iota = lax.broadcasted_iota(jnp.int32, (EDGE, EDGE), 1).astype(F32) + float(b * EDGE)
        parts.append(jnp.where(column == iota, 1.0, 0.0).astype(BF))
    return jnp.concatenate(parts, axis=1)


def push_kernel(u_ref, w_ref, rows_ref, out_ref, pushed, hot):
    pushed[...] = dot_nt(u_ref[...], w_ref[...]).astype(BF)
    per = hot.shape[0] // EDGE

    def step(i, carry):
        for j in range(per):
            hot[j * EDGE : (j + 1) * EDGE, :] = tall_onehot(
                rows_ref[pl.ds(i * per + j, 1), :], hot.shape[1]
            )
        start = pl.multiple_of(i * hot.shape[0], hot.shape[0])
        out_ref[pl.ds(start, hot.shape[0]), :] = dot_nn(hot[...], pushed[...]).astype(BF)
        return carry

    lax.fori_loop(0, out_ref.shape[0] // hot.shape[0], step, 0)


def push_rows(u, w, rows):
    masters, feat = u.shape
    total = rows.size
    return pl.pallas_call(
        push_kernel,
        out_shape=jax.ShapeDtypeStruct((total, feat), BF),
        scratch_shapes=[pltpu.VMEM((masters, feat), BF), pltpu.VMEM((1024, masters), BF)],
        compiler_params=params(),
        cost_estimate=pl.CostEstimate(
            flops=2 * total * masters * feat, bytes_accessed=total * feat * 2, transcendentals=0
        ),
        name="push_rows",
    )(u, w, rows.reshape(-1, EDGE))


def dense_kernel(rows_ref, cols_ref, count_ref, vals_ref, out_ref, acc):
    step = pl.program_id(0)
    per = vals_ref.shape[0]

    @pl.when(step == 0)
    def _():
        def clear(i, carry):
            acc[i] = jnp.zeros((EDGE, EDGE), F32)
            return carry

        lax.fori_loop(0, acc.shape[0], clear, 0)

    first = step * per
    live = jnp.clip(count_ref[0] - first, 0, per)

    def add(i, carry):
        at = rows_ref[first + i] * 16 + cols_ref[first + i]
        acc[at] += vals_ref[i].astype(F32)
        return carry

    lax.fori_loop(0, live, add, 0)

    @pl.when(step == pl.num_programs(0) - 1)
    def _():
        def flip(j, carry):
            start = pl.multiple_of(j * EDGE, EDGE)
            for i in range(16):
                block = jnp.transpose(acc[i * 16 + j]).astype(BF)
                lane = (i % 4) * EDGE
                out_ref[i // 4, pl.ds(start, EDGE), lane : lane + EDGE] = block
            return carry

        lax.fori_loop(0, 16, flip, 0)


def dense_adjacency(tile_vals, rows, cols, count):
    tiles = tile_vals.shape[0]
    per = 32
    return pl.pallas_call(
        dense_kernel,
        out_shape=jax.ShapeDtypeStruct((SLOTS // KSTEP, SLOTS, KSTEP), BF),
        grid_spec=pltpu.PrefetchScalarGridSpec(
            num_scalar_prefetch=3,
            grid=(tiles // per,),
            in_specs=[pl.BlockSpec((per, EDGE, EDGE), lambda i, *_: (i, 0, 0))],
            out_specs=pl.BlockSpec((SLOTS // KSTEP, SLOTS, KSTEP), lambda i, *_: (0, 0, 0)),
            scratch_shapes=[pltpu.VMEM((256, EDGE, EDGE), F32)],
        ),
        compiler_params=params(),
        cost_estimate=pl.CostEstimate(
            flops=tiles * EDGE * EDGE * 64, bytes_accessed=40 * 2**20, transcendentals=0
        ),
        name="dense_adjacency",
    )(rows, cols, count, tile_vals)


def spread_kernel(arrived_ref, slots_ref, slots_wide_ref, adj_hbm, out_ref, adj, acc, rows, sem):
    load = pltpu.make_async_copy(adj_hbm, adj, sem)
    load.start()
    acc[...] = jnp.zeros_like(acc)

    def place(k, carry):
        hot = wide_onehot(slots_wide_ref[pl.ds(k, 1), :], SLOTS)
        start = pl.multiple_of(k * KSTEP, KSTEP)
        acc[...] += dot_nn(hot, arrived_ref[pl.ds(start, KSTEP), :])
        return carry

    lax.fori_loop(0, arrived_ref.shape[0] // KSTEP, place, 0)
    rows[...] = acc[...].astype(BF)
    acc[...] = jnp.zeros_like(acc)
    load.wait()

    def multiply(k, carry):
        start = pl.multiple_of(k * KSTEP, KSTEP)
        acc[...] += dot_nn(adj[k], rows[pl.ds(start, KSTEP), :])
        return carry

    lax.fori_loop(0, SLOTS // KSTEP, multiply, 0)
    rows[...] = acc[...].astype(BF)
    per = 1024 // EDGE

    def collect(k, carry):
        hot = jnp.concatenate(
            [tall_onehot(slots_ref[pl.ds(k * per + j, 1), :], SLOTS) for j in range(per)], axis=0
        )
        start = pl.multiple_of(k * 1024, 1024)
        out_ref[pl.ds(start, 1024), :] = dot_nn(hot, rows[...]).astype(BF)
        return carry

    lax.fori_loop(0, out_ref.shape[0] // 1024, collect, 0)


def spread_rows(arrived, slots, adj):
    total, feat = arrived.shape
    vmem = pl.BlockSpec(memory_space=pltpu.VMEM)
    return pl.pallas_call(
        spread_kernel,
        out_shape=jax.ShapeDtypeStruct((total, feat), BF),
        in_specs=[vmem, vmem, vmem, pl.BlockSpec(memory_space=pl.ANY)],
        out_specs=vmem,
        scratch_shapes=[
            pltpu.VMEM(adj.shape, BF),
            pltpu.VMEM((SLOTS, feat), F32),
            pltpu.VMEM((SLOTS, feat), BF),
            pltpu.SemaphoreType.DMA,
        ],
        compiler_params=params(),
        cost_estimate=pl.CostEstimate(
            flops=4 * total * SLOTS * feat, bytes_accessed=14 * 2**20, transcendentals=0
        ),
        name="spread_rows",
    )(arrived, slots.reshape(-1, EDGE), slots.reshape(-1, KSTEP), adj)


def gather_kernel(masked, landed_ref, rows_ref, u_ref, w_ref, *rest):
    if masked:
        pre_ref, out_ref, acc = rest
    else:
        out_ref, acc = rest
    acc[...] = dot_nt(u_ref[...], w_ref[...])

    def step(k, carry):
        hot = wide_onehot(rows_ref[pl.ds(k, 1), :], acc.shape[0])
        start = pl.multiple_of(k * KSTEP, KSTEP)
        acc[...] += dot_nn(hot, landed_ref[pl.ds(start, KSTEP), :])
        return carry

    lax.fori_loop(0, landed_ref.shape[0] // KSTEP, step, 0)
    if masked:
        out_ref[...] = jnp.where(pre_ref[...].astype(F32) > 0.0, acc[...], 0.0).astype(BF)
    else:
        out_ref[...] = acc[...].astype(BF)


def gather_back(landed, rows, u, w, preact):
    args = [landed, rows.reshape(-1, KSTEP), u, w] + ([] if preact is None else [preact])
    total, feat = landed.shape
    return pl.pallas_call(
        functools.partial(gather_kernel, preact is not None),
        out_shape=jax.ShapeDtypeStruct(u.shape, BF),
        scratch_shapes=[pltpu.VMEM(u.shape, F32)],
        compiler_params=params(),
        cost_estimate=pl.CostEstimate(
            flops=2 * total * u.shape[0] * feat, bytes_accessed=total * feat * 2, transcendentals=0
        ),
        name="gather_back",
    )(*args)


def on_device(
    features,
    preact,
    agg_first,
    agg_second,
    grad_out,
    self_first,
    neigh_first,
    self_second,
    neigh_second,
    tile_vals,
    tile_rows,
    tile_cols,
    tile_count,
    send_count,
    mirror_slot,
    master_row,
):
    domains = lax.axis_size("dom")
    groups = lax.axis_size("group")
    masters, feat = features.shape
    factor = (masters * domains * groups) ** (-0.5)
    capacity = mirror_slot.shape[2]
    rows = master_row[0].astype(F32)
    live = jnp.arange(capacity)[None, :] < send_count[0][:, None]
    slots = jnp.where(live, mirror_slot[0], -1).astype(F32)

    def swap(x, axis="dom"):
        return lax.all_to_all(x, axis, split_axis=0, concat_axis=0, tiled=True)

    def swap_rows(x):
        return swap(x.reshape(domains, capacity, feat)).reshape(-1, feat)

    def grads(inputs, stored, upstream):
        both = [
            jnp.einsum("nf,ng->fg", part, upstream, preferred_element_type=F32)
            for part in (inputs, stored)
        ]
        return jnp.concatenate(both, axis=0) * factor

    def sum_everywhere(total):
        height = total.shape[0] // groups
        part = jnp.sum(swap(total.reshape(groups, height, feat), "group"), axis=0)
        piece = jnp.sum(swap(part.reshape(domains, height // domains, feat)), axis=0)
        part = swap(jnp.broadcast_to(piece, (domains,) + piece.shape)).reshape(height, feat)
        return swap(jnp.broadcast_to(part, (groups,) + part.shape), "group").reshape(-1, feat)

    activated = jnp.maximum(preact, 0.0)
    arrived = swap_rows(push_rows(grad_out, neigh_second, rows))
    adj = dense_adjacency(tile_vals, tile_rows[0], tile_cols[0], tile_count)
    weights_two = lax.psum(grads(activated, agg_second, grad_out), ("group", "dom"))
    landed = swap_rows(spread_rows(arrived, slots, adj))
    upstream = gather_back(landed, rows, grad_out, self_second, preact)

    arrived = swap_rows(push_rows(upstream, neigh_first, rows))
    weights_one = sum_everywhere(grads(features, agg_first, upstream))
    landed = swap_rows(spread_rows(arrived, slots, adj))
    input_grad = gather_back(landed, rows, upstream, self_first, None)
    weight_grads = jnp.concatenate([weights_one, weights_two], axis=0).reshape(4, feat, feat)
    return (input_grad, weight_grads)


def solution(mesh):
    every = ("group", "dom")
    in_specs = (
        (P(every, None),) * 5
        + (P(),) * 4
        + (P(every, None, None), P(every, None), P(every, None), P(every), P(every, None))
        + (P(every, None, None),) * 2
    )
    out_specs = (P(every, None), P())
    return jax.shard_map(
        on_device, mesh=mesh, in_specs=in_specs, out_specs=out_specs, check_vma=False
    )
```

time: 1140 us -> 663 us (0.58)
  other arithmetic: 248 us -> 6.54 us
  local copies, waits for them, and re-layouts: 219 us -> 8.5 us
  matrix products: 105 us -> 5.03 us
  Pallas kernels: 0 us -> 88.9 us
  starting transfers between devices: 82.7 us -> 38.3 us
  blocking collectives: 0 us -> 29.8 us
    scatter-add x22 -> x0, other arithmetic: 201 us -> none  [the longest x20 130 us: visit(): return running.at[targets].add(product, mode='drop')]
    gather x24 -> x0, local copies, waits for them, and re-layouts: 140 us -> none  [the longest x2 50.2 us: mirror_round(): outgoing = pushed[row_list]]
    dot_general x28 -> x4, matrix products: 105 us -> 5.03 us  [grads(): jnp.einsum('nf,ng->fg', part, upstream, preferred_element_type=F32)]
    pallas_call x0 -> x7, Pallas kernels: none -> 88.9 us  [the longest x2 46.5 us: spread_rows(): pl.pallas_call(spread_kernel, out_shape=jax.ShapeDtypeStruct((total, feat...]
    scatter x2 -> x0, local copies, waits for them, and re-layouts: 53.9 us -> none  [mirror_round(): mirrored = jnp.zeros((SLOTS, feat_width), jnp.bfloat16).at[slot_index.res...]
    all_to_all x4 -> x6, starting transfers between devices: 82.7 us -> 38.3 us  [swap(): return lax.all_to_all(x, axis, split_axis=0, concat_axis=0, tiled=True)]
    select_n x26 -> x0, other arithmetic: 40 us -> none  [the longest x20 28.5 us: visit(): picked = blocks[row_block]]
    all_to_all x0 -> x2, blocking collectives: none -> 29.8 us  [swap(): return lax.all_to_all(x, axis, split_axis=0, concat_axis=0, tiled=True)]
  transfers between devices with their start and end apart: 5 -> 7, of which waited for: 4 -> 5; matrix products, arithmetic and copies ran while one was open for 3% -> 1% of each run, Pallas kernels for 0% -> 7%
where the time goes in v1:
time: 663 us; the launch traced here: 662 us
  waiting for transfers between devices  470 us (71%)
  Pallas kernels  88.9 us (13%)
  starting transfers between devices  38.3 us (6%)
  blocking collectives  29.8 us (4%)
  between operations  14.9 us (2%)
  local copies, waits for them, and re-layouts  8.5 us (1%)
    psum x1, waiting for transfers between devices, on_device(): lax.psum(grads(activated, agg_second, grad_out), ('group', 'dom'))  272 us
    all_to_all x6, waiting for transfers between devices, swap(): return lax.all_to_all(x, axis, split_axis=0, concat_axis=0, tiled=True)  198 us
    pallas_call x2, Pallas kernels, spread_rows(): pl.pallas_call(spread_kernel, out_shape=jax.ShapeDtypeStruct((total, feat...  46.5 us
    all_to_all x6, starting transfers between devices, swap(): return lax.all_to_all(x, axis, split_axis=0, concat_axis=0, tiled=True)  38.3 us
    all_to_all x2, blocking collectives, swap(): return lax.all_to_all(x, axis, split_axis=0, concat_axis=0, tiled=True)  29.8 us
    pallas_call x1, Pallas kernels, dense_adjacency(): pl.pallas_call(dense_kernel, out_shape=jax.ShapeDtypeStruct((SLOTS // KST...  17.3 us
    pallas_call x2, Pallas kernels, gather_back(): pl.pallas_call(functools.partial(gather_kernel, preact is not None), out_...  13.3 us
  transfers between devices with their start and end apart: 7, of which 5 were waited for; matrix products, arithmetic and copies ran while one was open for 1% of the time, Pallas kernels for 7%

profile of v1, /device:TPU:8, one launch (start us, length us, event | category | flops | bytes accessed | tf_op | source)
XLA Modules:
  0.0 662.1 jit_solution(8478380007703632363)
XLA Ops:
  8.7 5.9 push_rows.2
  14.6 11.5 %all-to-all-start = ((bf16[32,192,256]{2,1,0:T(8,128)(2,1)}), bf16[32,192,256]{2,1,0:T(8,128)(2,1)S(1)}, u32[]{:S(2)}, u32[]{:S(2)}) async-start(bf16[32,192,256]{2,1,0:T(8,128)(2,1)} %bitcast.26), calls=%async_computation | async-start | bytes 6291456 | tf_op jit(solution)/shard_map/all_to_all | solution.py:252
  28.4 17.3 %dense_adjacency.1.adj_hbm = bf16[4,2048,512]{2,1,0:T(8,128)(2,1)} custom-call(s32[384]{0:T(512)} %reduce.rows_ref, s32[384]{0:T(512)} %reduce.1.cols_ref, s32[1]{0:T(128)S(6)} %copy.21.count_ref, bf16[384,128,128]{2,1,0:T(8,128)(2,1)} %vals_ref.1), custom_call_target="tpu_custom_call" | custom-call | flops 402653184 | bytes 41943040 | tf_op jit(solution)/shard_map/dense_adjacency/pallas_call | solution.py:113
  46.9 51.4 %all-to-all-done = bf16[32,192,256]{2,1,0:T(8,128)(2,1)S(1)} async-done(((bf16[32,192,256]{2,1,0:T(8,128)(2,1)}), bf16[32,192,256]{2,1,0:T(8,128)(2,1)S(1)}, u32[]{:S(2)}, u32[]{:S(2)}) %all-to-all-start) | async-done | bytes 3145760 | tf_op jit(solution)/shard_map/all_to_all | solution.py:252
  98.4 1.7 copy-done.2
  100.1 23.2 %spread_rows.2 = bf16[6144,256]{1,0:T(8,128)(2,1)} custom-call(bf16[6144,256]{1,0:T(8,128)(2,1)} %bitcast.25, f32[48,128]{1,0:T(8,128)} %select_convert_fusion.1.slots_ref, f32[12,512]{1,0:T(8,128)} %select_convert_fusion.slots_wide_ref, bf16[4,2048,512]{2,1,0:T(8,128)(2,1)} %dense_adjacency.1.adj_hbm), custom_call_target="tpu_custom_call" | custom-call | flops 12884901888 | bytes 14680064 | tf_op jit(solution)/shard_map/spread_rows/pallas_call | solution.py:170
  123.3 6.3 all-to-all-start.1
  130.3 71.2 %all-to-all-done.1 = bf16[32,192,256]{2,1,0:T(8,128)(2,1)S(1)} async-done(((bf16[32,192,256]{2,1,0:T(8,128)(2,1)}), bf16[32,192,256]{2,1,0:T(8,128)(2,1)S(1)}, u32[]{:S(2)}, u32[]{:S(2)}) %all-to-all-start.1) | async-done | bytes 3145760 | tf_op jit(solution)/shard_map/all_to_all | solution.py:252
  201.6 1.7 copy-done.4
  203.3 6.8 %gather_back.2.u_ref = bf16[512,256]{1,0:T(8,128)(2,1)} custom-call(bf16[6144,256]{1,0:T(8,128)(2,1)} %bitcast.29, f32[12,512]{1,0:T(8,128)} %convert_element_type.22.rows_ref, bf16[512,256]{1,0:T(8,128)(2,1)} %u_ref.3, bf16[256,256]{1,0:T(8,128)(2,1)} %w_ref.5, bf16[512,256]{1,0:T(8,128)(2,1)} %rest_0_.1), custom_call_target="tpu_custom_call" | custom-call | flops 1610612736 | bytes 3145728 | tf_op jit(solution)/shard_map/gather_back/pallas_call | solution.py:212
  212.6 13.7 %all_to_all.40 = f32[8,64,256]{2,1,0:T(8,128)S(1)} all-to-all(f32[8,64,256]{2,1,0:T(8,128)S(1)} %bitcast.31), channel_id=1, replica_groups=mesh['group'=8,'dom'=32] {'group'}, dimensions={0} | all-to-all | bytes 1048576 | tf_op jit(solution)/shard_map/all_to_all | solution.py:252
  226.4 16.1 %all_to_all.41 = f32[32,2,256]{2,1,0:T(2,128)S(1)} all-to-all(f32[32,2,256]{2,1,0:T(2,128)S(1)} %reshape.73), channel_id=1, replica_groups=mesh['group'=8,'dom'=32] {'dom'}, dimensions={0} | all-to-all | bytes 131072 | tf_op jit(solution)/shard_map/all_to_all | solution.py:252
  243.2 3.9 all-to-all-start.6
  247.0 5.9 push_rows.3
  253.0 4.1 all-to-all-done.6
  257.1 5.7 all-to-all-start.2
  262.8 71.3 %all-to-all-done.2 = bf16[32,192,256]{2,1,0:T(8,128)(2,1)S(1)} async-done(((bf16[32,192,256]{2,1,0:T(8,128)(2,1)}), bf16[32,192,256]{2,1,0:T(8,128)(2,1)S(1)}, u32[]{:S(2)}, u32[]{:S(2)}) %all-to-all-start.2) | async-done | bytes 3145760 | tf_op jit(solution)/shard_map/all_to_all | solution.py:252
  335.0 5.5 all-to-all-start.7
  340.5 23.2 %spread_rows.3 = bf16[6144,256]{1,0:T(8,128)(2,1)} custom-call(bf16[6144,256]{1,0:T(8,128)(2,1)} %bitcast.27, f32[48,128]{1,0:T(8,128)} %select_convert_fusion.1.slots_ref, f32[12,512]{1,0:T(8,128)} %select_convert_fusion.slots_wide_ref, bf16[4,2048,512]{2,1,0:T(8,128)(2,1)} %dense_adjacency.1.adj_hbm), custom_call_target="tpu_custom_call" | custom-call | flops 12884901888 | bytes 14680064 | tf_op jit(solution)/shard_map/spread_rows/pallas_call | solution.py:170
  363.8 5.4 all-to-all-start.3
  372.7 272.1 %all-reduce.2.cloned.1.call-done = f32[512,256]{1,0:T(8,128)} async-done(((f32[512,256]{1,0:T(8,128)}), f32[512,256]{1,0:T(8,128)}) %all-reduce.2.cloned.1.call-update) | async-done | bytes 524304 | tf_op jit(solution)/shard_map/psum | solution.py:274
  644.9 2.2 pad_maximum_fusion
  647.1 1.6 copy-done.1
  648.7 6.5 gather_back.3
  (45 shorter events, 12.8 us)
Async XLA Ops:
  7.2 202.9 %copy-start = (bf16[512,256]{1,0:T(8,128)(2,1)S(1)}, bf16[512,256]{1,0:T(8,128)(2,1)}, u32[]{:S(2)}) copy-start(bf16[512,256]{1,0:T(8,128)(2,1)} %param.18) | copy-start | bytes 786436
  14.6 11.5 %copy-start.9 = (s32[1,32]{1,0:T(1,128)S(1)}, s32[1,32]{1,0:T(1,128)}, u32[]{:S(2)}) copy-start(s32[1,32]{1,0:T(1,128)} %param.29) | copy-start | bytes 388
  14.6 11.8 %copy-start.6 = (s32[1,32,192]{2,1,0:T(8,128)S(1)}, s32[1,32,192]{2,1,0:T(8,128)}, u32[]{:S(2)}) copy-start(s32[1,32,192]{2,1,0:T(8,128)} %param.30) | copy-start | bytes 73732
  14.6 11.9 %copy-start.7 = (s32[1,384]{1,0:T(1,128)S(1)}, s32[1,384]{1,0:T(1,128)}, u32[]{:S(2)}) copy-start(s32[1,384]{1,0:T(1,128)} %param.26) | copy-start | bytes 4612
  14.6 12.5 %copy-start.8 = (s32[1,384]{1,0:T(1,128)S(1)}, s32[1,384]{1,0:T(1,128)}, u32[]{:S(2)}) copy-start(s32[1,384]{1,0:T(1,128)} %param.27) | copy-start | bytes 4612
  14.6 83.7 %all-to-all-start = ((bf16[32,192,256]{2,1,0:T(8,128)(2,1)}), bf16[32,192,256]{2,1,0:T(8,128)(2,1)S(1)}, u32[]{:S(2)}, u32[]{:S(2)}) async-start(bf16[32,192,256]{2,1,0:T(8,128)(2,1)} %bitcast.26), calls=%async_computation | async-start | bytes 6291456 | tf_op jit(solution)/shard_map/all_to_all | solution.py:252
  98.4 1.7 copy-start.2
  123.3 78.2 %all-to-all-start.1 = ((bf16[32,192,256]{2,1,0:T(8,128)(2,1)}), bf16[32,192,256]{2,1,0:T(8,128)(2,1)S(1)}, u32[]{:S(2)}, u32[]{:S(2)}) async-start(bf16[32,192,256]{2,1,0:T(8,128)(2,1)} %bitcast.30), calls=%async_computation.1 | async-start | bytes 6291456 | tf_op jit(solution)/shard_map/all_to_all | solution.py:252
  201.6 1.7 copy-start.4
  203.3 8.0 %copy-start.5 = (bf16[512,256]{1,0:T(8,128)(2,1)S(1)}, bf16[512,256]{1,0:T(8,128)(2,1)}, u32[]{:S(2)}) copy-start(bf16[512,256]{1,0:T(8,128)(2,1)} %param.16) | copy-start | bytes 786436
  243.2 13.9 %all-to-all-start.6 = ((f32[32,2,256]{2,1,0:T(2,128)}), f32[32,2,256]{2,1,0:T(2,128)S(1)}, u32[]{:S(2)}, u32[]{:S(2)}) async-start(f32[32,2,256]{2,1,0:T(2,128)} %broadcast_in_dim.15), calls=%async_computation.6 | async-start | bytes 131072 | tf_op jit(solution)/shard_map/all_to_all | solution.py:252
  257.1 77.0 %all-to-all-start.2 = ((bf16[32,192,256]{2,1,0:T(8,128)(2,1)}), bf16[32,192,256]{2,1,0:T(8,128)(2,1)S(1)}, u32[]{:S(2)}, u32[]{:S(2)}) async-start(bf16[32,192,256]{2,1,0:T(8,128)(2,1)} %bitcast.28), calls=%async_computation.2 | async-start | bytes 6291456 | tf_op jit(solution)/shard_map/all_to_all | solution.py:252
  334.1 6.4 copy-start.3
  335.0 28.8 %all-to-all-start.7 = ((f32[8,64,256]{2,1,0:T(8,128)}), f32[8,64,256]{2,1,0:T(8,128)}, u32[]{:S(2)}, u32[]{:S(2)}) async-start(f32[8,64,256]{2,1,0:T(8,128)} %broadcast_in_dim.16), calls=%async_computation.7 | async-start | bytes 1048576 | tf_op jit(solution)/shard_map/all_to_all | solution.py:252
  363.8 283.3 %all-to-all-start.3 = ((bf16[32,192,256]{2,1,0:T(8,128)(2,1)}), bf16[32,192,256]{2,1,0:T(8,128)(2,1)S(1)}, u32[]{:S(2)}, u32[]{:S(2)}) async-start(bf16[32,192,256]{2,1,0:T(8,128)(2,1)} %bitcast.23), calls=%async_computation.3 | async-start | bytes 6291456 | tf_op jit(solution)/shard_map/all_to_all | solution.py:252
  369.2 275.7 %all-reduce.2.cloned.1.call-start = ((), (), s32[]{:S(2)}) async-start(), calls=%async_computation.8 | async-start | bytes 1048576 | tf_op jit(solution)/shard_map/psum | solution.py:274
  647.1 1.6 copy-start.1
Sparse Core Ops, SparseCore 0:
  376.1 268.7 all-reduce.1
